TPU v7x, 256 devices: a whole 4x4x8 slice. The times are simulated.
256 devices in a mesh: gy: 32 (over y, z), gx: 8 (over x, core).
Axes of the slice: x: 4, y: 4, z: 8, core: 2. Of those that a mesh axis runs over, the one named last changes fastest.
Arguments:
- spatial_grad: float32 [3, 256, 128, 128], P(None, 'gy', 'gx'), may hold values from -4 to 4
- temporal_grad: float32 [256, 128, 128], P('gy', 'gx'), may hold values from -6 to 6
Outputs:
- flow: float32 [3, 256, 128, 128], P(None, 'gy', 'gx')
All inputs are finite; a program needn't handle non-finite values.
Results may differ from a plain program's by a relative error of at most 0.0001.
Values sent between devices are 32-bit elements; how exact they have to be, the bound alone decides.
A program may use at most 192 MiB of HBM per device.

v0:
```python
import functools

import jax
import jax.numpy as jnp
from jax import lax
from jax.experimental import pallas as pl
from jax.experimental.pallas import tpu as pltpu
from jax.sharding import PartitionSpec as P

MESH = pl.DeviceIdType.MESH
F32 = jnp.float32
BF16 = jnp.bfloat16
KEEP = 0.2
DAMP = 0.8
W = (1.0, 0.25, 0.0625, 0.015625)

NEAR = [(a, b) for a in (-1, 0, 1) for b in (-1, 0, 1) if (a, b) != (0, 0)]
OUTER = [(a, b) for a in (-2, 2) for b in (-1, 0, 1)]
BOX = NEAR + OUTER
RING4 = [1, -1, 2, -2, 3, -3, 4, -4]
RING11 = [s * d for d in range(1, 12) for s in (1, -1)]


def loop(first, last, body):
    def step(i, carry):
        body(i)
        return carry

    lax.fori_loop(first, last, step, 0)


def iota(shape, dim):
    return lax.broadcasted_iota(jnp.int32, shape, dim)


def roll(x, shift, axis):
    return pltpu.roll(x, shift % x.shape[axis], axis)


def split_dot(x, matrix):
    high = x.astype(BF16).astype(F32)
    both = jnp.concatenate([high, x - high], axis=0).astype(BF16)
    out = jnp.dot(both, matrix, preferred_element_type=F32)
    rows = x.shape[0]
    return out[:rows] + out[rows:]


def fold_weight(d):
    return jnp.where((d == 0) | (d == 1), 3.0, jnp.where((d == -1) | (d == 2), 1.0, 0.0))


def spread_weight(d):
    return jnp.where((d == 0) | (d == 1), 0.75, jnp.where((d == -1) | (d == 2), 0.25, 0.0))


def sym(m, v):
    return [
        m[0] * v[0] + m[3] * v[1] + m[4] * v[2],
        m[3] * v[0] + m[1] * v[1] + m[5] * v[2],
        m[4] * v[0] + m[5] * v[1] + m[2] * v[2],
    ]


def damped_inverse(m, weight, mask):
    dx, dy, dz = (m[k] + 6.0 * weight for k in range(3))
    xy, xz, yz = m[3], m[4], m[5]
    cof = [
        dy * dz - yz * yz,
        dx * dz - xz * xz,
        dx * dy - xy * xy,
        xz * yz - xy * dz,
        xy * yz - dy * xz,
        xy * xz - dx * yz,
    ]
    det = dx * cof[0] + xy * cof[3] + xz * cof[4]
    scale = mask * DAMP / det
    return [c * scale for c in cof]


def kernel(
    sg, tg, out,
    IN, Q, VA, VB, R0, XM0, FS, CZ, TMP,
    RA1, A1, I1, RS1, S1, V1A, V1B, R1, XM1,
    C1, C2, F, XA, A2, I2, XG, S2, V2A, V2B, YM2, E21, P21,
    RA3, I3, SG, V3, E3, P3,
    M01, M12, M23, P01, P12, P23, M32, M21, M10,
    lsem, ssem, rsem,
):
    gy = lax.axis_index("gy")
    gx = lax.axis_index("gx")

    def at(dy, dx):
        return lax.rem(gy + dy + 32, 32), lax.rem(gx + dx + 8, 8)

    barrier = pltpu.get_barrier_semaphore()
    everyone = BOX + [(d, 0) for d in RING11 if abs(d) > 2] + [(0, d) for d in (2, 3, 4, 5, 6)]
    for peer in everyone:
        pl.semaphore_signal(barrier, inc=1, device_id=at(*peer), device_id_type=MESH)

    load_g = pltpu.make_async_copy(sg, IN.at[0:3, 7:15, 8:24], lsem.at[0])
    load_t = pltpu.make_async_copy(tg, IN.at[3, 7:15, 8:24], lsem.at[1])
    load_g.start()
    load_t.start()

    count = [0]

    def send(src, dst, peer):
        k = count[0]
        count[0] += 1
        copy = pltpu.make_async_remote_copy(
            src_ref=src, dst_ref=dst, send_sem=ssem.at[k], recv_sem=rsem.at[k],
            device_id=at(*peer), device_id_type=MESH,
        )
        copy.start()
        return copy

    def received(copies):
        for copy in copies:
            copy.wait_recv()

    sent = []

    def lanes(shape):
        return iota(shape, 0), iota(shape, 1)

    k, n = lanes((128, 128))
    M01[...] = (fold_weight(k - 2 * (n & 63)) * (1.0 / 512.0)).astype(BF16)
    P01[...] = jnp.where((k >> 1) == (n & 63), 0.125, 0.0).astype(BF16)
    M12[...] = jnp.where(k < 64, fold_weight(k - 2 * (n & 31)) * (1.0 / 512.0), 0.0).astype(BF16)
    P12[...] = jnp.where((k < 64) & ((k >> 1) == (n & 31)), 0.125, 0.0).astype(BF16)
    part = (n & 31) >> 4
    M23[...] = jnp.where(
        (k >> 5) == 2 * part, fold_weight((k & 31) - 2 * (n & 15)) * (1.0 / 512.0), 0.0
    ).astype(BF16)
    P23[...] = jnp.where(((k >> 6) == part) & (((k & 31) >> 1) == (n & 15)), 0.125, 0.0).astype(BF16)
    M10[...] = jnp.where(k < 64, spread_weight(n - 2 * k), 0.0).astype(BF16)
    for q in range(4):
        M21[:, 128 * q:128 * q + 128] = jnp.where(
            ((k >> 5) == q) & (n < 64), spread_weight(n - 2 * (k & 31)), 0.0
        ).astype(BF16)
        for eo in range(2):
            xs = n >> 5
            fits = ((xs & 1) == eo) & ((k >> 4) == 2 * q + (xs >> 1))
            M32[eo, :, 128 * q:128 * q + 128] = jnp.where(
                fits, spread_weight((n & 31) - 2 * (k & 15)), 0.0
            ).astype(BF16)

    row = iota((32, 128), 0) + (16 * gx - 8)
    XM0[...] = jnp.where((row >= 0) & (row < 128), 1.0, 0.0)
    row = iota((24, 128), 0) + (8 * gx - 8)
    XM1[...] = jnp.where((row >= 0) & (row < 64) & (iota((24, 128), 1) < 64), 1.0, 0.0)
    plane = iota((18, 8, 128), 0) + (2 * gy - 8)
    YM2[...] = jnp.where((plane >= 0) & (plane < 64), 1.0, 0.0)
    E21[...] = jnp.zeros_like(E21)
    SG[:, 0:8] = jnp.zeros((2, 8, 128), F32)
    RA3[0:16] = jnp.zeros((16, 128), F32)

    def ym(first, length, y):
        place = first + y
        return jnp.where((place >= 0) & (place < length), 1.0, 0.0).astype(F32)

    def ym0(y):
        return ym(8 * gy - 7, 256, y)

    def ym1(y):
        return ym(4 * gy - 8, 128, y)

    def pack(rows, group):
        size = rows.shape[0]
        keep = (iota(rows.shape, 1) >> 5) == (iota(rows.shape, 0) & 3)
        F[0:size] = jnp.where(keep, rows, 0.0)
        kept = 8 * ((size // group + 7) // 8)
        total = F[pl.ds(0, kept, stride=group)]
        for r in range(1, group):
            total = total + F[pl.ds(r, kept, stride=group)]
        return total

    F[...] = jnp.zeros_like(F)

    load_g.wait()
    load_t.wait()

    def own_coeffs(i):
        def products(y):
            g = [IN[c, y, 8:24] for c in range(3)]
            return [g[0] * g[0], g[1] * g[1], g[2] * g[2], g[0] * g[1], g[0] * g[2], g[1] * g[2]]

        one, two = products(7 + 2 * i), products(8 + 2 * i)
        for f in range(6):
            FS[f, 0:16] = one[f] + two[f]
        for f in range(6):
            C1[pl.ds(f * 32 + 8 * i, 8)] = FS[f, pl.ds(0, 8, stride=2)] + FS[f, pl.ds(1, 8, stride=2)]

    loop(0, 4, own_coeffs)
    C2[...] = split_dot(C1[...], P01[...])
    low = iota((8, 128), 1) < 64
    for f in range(6):
        for j in range(2):
            RA1[2, 1, f, j] = jnp.where(
                low, C2[32 * f + 8 * j:32 * f + 8 * j + 8], C2[32 * f + 8 * j + 16:32 * f + 8 * j + 24]
            )
    halved = C2[pl.ds(0, 96, stride=2)] + C2[pl.ds(1, 96, stride=2)]
    XA[pl.ds(pl.multiple_of(gx * 16, 16), 16)] = pack(split_dot(halved, P12[...]), 8)

    pl.semaphore_wait(barrier, len(everyone))

    span = {-1: (0, 8, 24), 0: (0, 16, 8), 1: (8, 8, 0)}

    def input_copy(peer, rows):
        dy, dx = peer
        x0, width, to = span[dx]
        if dy == 0:
            y0, height, y1 = 0, 8, 7
        elif rows == "near":
            height = 3
            y0, y1 = (5, 4) if dy == 1 else (0, 15)
        else:
            height = 4
            y0, y1 = (1, 0) if dy == 1 else (3, 18)
        return send(
            IN.at[:, 7 + y0:7 + y0 + height, 8 + x0:8 + x0 + width],
            IN.at[:, y1:y1 + height, to:to + width],
            peer,
        )

    near_in = [input_copy(peer, "near") for peer in NEAR]
    a2_x = [
        send(XA.at[pl.ds(pl.multiple_of(gx * 16, 16), 16)], XA.at[pl.ds(pl.multiple_of(gx * 16, 16), 16)], (0, d))
        for d in range(1, 8)
    ]
    a1_in = {peer: send(RA1.at[2, 1], RA1.at[2 - peer[0], 1 - peer[1]], peer) for peer in BOX}
    far_in = [input_copy(peer, "far") for peer in NEAR if peer[0] != 0]
    sent += near_in + a2_x + list(a1_in.values()) + far_in
    received(near_in)

    lane0 = iota((32, 128), 1)
    first_lane, last_lane = lane0 == 0, lane0 == 127

    def around0(src, y):
        centre, total = [], []
        for c in range(3):
            v = src[c, y]
            n = src[c, y - 1] + src[c, y + 1]
            n = n + (roll(v, 1, 0) + roll(v, -1, 0))
            n = n + jnp.where(first_lane, 0.0, roll(v, 1, 1)) + jnp.where(last_lane, 0.0, roll(v, -1, 1))
            centre.append(v)
            total.append(n)
        return centre, total

    def dot3(a, b):
        return a[0] * b[0] + a[1] * b[1] + a[2] * b[2]

    def start0(y):
        g = [IN[c, y] for c in range(3)]
        q = XM0[...] * ym0(y) * (DAMP / 6.0) / (6.0 + dot3(g, g))
        Q[y] = q
        scale = -6.0 * IN[3, y] * q
        for c in range(3):
            VA[c, y] = scale * g[c]

    def swept0(src, y):
        g = [IN[c, y] for c in range(3)]
        t = IN[3, y]
        v, n = around0(src, y)
        p = [n[c] - t * g[c] for c in range(3)]
        d = dot3(g, p) * Q[y]
        scale = XM0[...] * (ym0(y) * (DAMP / 6.0))
        return [KEEP * v[c] + scale * p[c] - d * g[c] for c in range(3)]

    def sweep0(src, dst, first, last):
        def body(y):
            new = swept0(src, y)
            for c in range(3):
                dst[c, y] = new[c]

        loop(first, last, body)

    def residue0(src):
        def body(y):
            g = [IN[c, y] for c in range(3)]
            v, n = around0(src, y)
            d = IN[3, y] + dot3(g, v)
            m = XM0[...] * ym0(y)
            for c in range(3):
                R0[c, y - 6] = m * (n[c] - 6.0 * v[c] - g[c] * d)

        loop(6, 16, body)

    def fold_rows(src, c, y, x, size):
        weights = (1.0, 3.0, 3.0, 1.0)
        total = None
        for kx in range(4):
            line = None
            for ky in range(4):
                term = src[c, y + ky, pl.ds(x + kx, size, stride=2)]
                term = term if weights[ky] == 1.0 else weights[ky] * term
                line = term if line is None else line + term
            line = line if weights[kx] == 1.0 else weights[kx] * line
            total = line if total is None else total + line
        return total

    def source1(cycle):
        def body(i):
            for c in range(3):
                C1[pl.ds(c * 32 + 8 * i, 8)] = fold_rows(R0, c, 2 * i, 7, 8)

        loop(0, 4, body)
        s = split_dot(C1[0:96], M01[...])
        for c in range(3):
            for j in range(2):
                at0 = 32 * c + 8 * j
                RS1[cycle, 2, 1, c, j] = jnp.where(low, s[at0:at0 + 8], s[at0 + 16:at0 + 24])

    low4 = iota((3, 2, 8, 128), 3) < 64
    low6 = iota((6, 2, 8, 128), 3) < 64

    def unpack(src, dst, mask, group):
        for dx in range(3):
            p = src[group, dx]
            other = pltpu.roll(p.reshape(-1, 128), 64, 1).reshape(p.shape)
            dst[:, pl.ds(4 * group, 2), 8 * dx:8 * dx + 8] = jnp.where(mask, p, 0.0)
            dst[:, pl.ds(4 * group + 2, 2), 8 * dx:8 * dx + 8] = jnp.where(mask, other, 0.0)

    def inverse1(y):
        m = damped_inverse([A1[f, y] for f in range(6)], W[1], XM1[...] * ym1(y))
        for f in range(6):
            I1[f, y] = m[f]

    def around1(src, y):
        centre, total = [], []
        for c in range(3):
            v = src[c, y]
            n = src[c, y - 1] + src[c, y + 1]
            n = n + (roll(v, 1, 0) + roll(v, -1, 0)) + (roll(v, 1, 1) + roll(v, -1, 1))
            centre.append(v)
            total.append(n)
        return centre, total

    def start1(y):
        new = sym([I1[f, y] for f in range(6)], [S1[c, y] for c in range(3)])
        for c in range(3):
            V1A[c, y] = new[c]

    def sweep1(src, dst, first, last):
        def body(y):
            v, n = around1(src, y)
            new = sym([I1[f, y] for f in range(6)], [S1[c, y] + W[1] * n[c] for c in range(3)])
            for c in range(3):
                dst[c, y] = KEEP * v[c] + new[c]

        loop(first, last, body)

    def residue1(src):
        def body(y):
            v, n = around1(src, y)
            av = sym([A1[f, y] for f in range(6)], v)
            m = XM1[...] * ym1(y)
            for c in range(3):
                R1[c, y - 7] = m * (S1[c, y] + W[1] * (n[c] - 6.0 * v[c]) - av[c])

        loop(7, 13, body)

    def source2(cycle):
        rows = []
        for c in range(3):
            for i in range(2):
                FS[0, 4 * (2 * c + i):4 * (2 * c + i) + 4] = fold_rows(R1, c, 2 * i, 7, 4)
        XG[cycle, pl.ds(pl.multiple_of(gx * 8, 8), 8)] = pack(split_dot(FS[0, 0:24], M12[...]), 4)

    def shifts2(v):
        lane, r = iota(v.shape, 1), iota(v.shape, 0) & 7
        up = roll(v, -32, 1)
        xp = jnp.where(lane < 96, up, jnp.where(r == 7, 0.0, roll(up, -1, 0)))
        down = roll(v, 32, 1)
        xm = jnp.where(lane >= 32, down, jnp.where(r == 0, 0.0, roll(down, 1, 0)))
        return xm, xp

    def around2(src, first, last):
        centre, total = [], []
        for c in range(3):
            v3 = src[c, first:last]
            v = v3.reshape(-1, 128)
            z = iota(v.shape, 1) & 31
            xm, xp = shifts2(v)
            n = xm + xp + jnp.where(z == 0, 0.0, roll(v, 1, 1)) + jnp.where(z == 31, 0.0, roll(v, -1, 1))
            n = n.reshape(v3.shape) + (src[c, first - 1:last - 1] + src[c, first + 1:last + 1])
            centre.append(v3)
            total.append(n)
        return centre, total

    def start2(cycle, first, last):
        new = sym([I2[f, first:last] for f in range(6)], [S2[cycle, c, first:last] for c in range(3)])
        for c in range(3):
            V2A[c, first:last] = new[c]

    def sweep2(cycle, src, dst, first, last):
        v, n = around2(src, first, last)
        p = [S2[cycle, c, first:last] + W[2] * n[c] for c in range(3)]
        new = sym([I2[f, first:last] for f in range(6)], p)
        for c in range(3):
            dst[c, first:last] = KEEP * v[c] + new[c]

    def source3(cycle):
        v, n = around2(V2B, 7, 11)
        av = sym([A2[f, 7:11] for f in range(6)], v)
        rows = []
        for c in range(3):
            r = YM2[7:11] * (S2[cycle, c, 7:11] + W[2] * (n[c] - 6.0 * v[c]) - av[c])
            f = r[0] + 3.0 * (r[1] + r[2]) + r[3]
            xm, xp = shifts2(f)
            _, more = shifts2(3.0 * f + xp)
            rows.append(xm + 3.0 * f + more)
        SG[cycle, 96:104] = pack(split_dot(jnp.concatenate(rows, axis=0), M23[...]), 4)

    lane3 = iota((24, 128), 1)

    def shifts3(a, b):
        ua, ub = roll(a, -16, 1), roll(b, -16, 1)
        da, db = roll(a, 16, 1), roll(b, 16, 1)
        up = jnp.where(lane3 < 112, ua, ub), jnp.where(lane3 < 112, ub, 0.0)
        down = jnp.where(lane3 >= 16, da, 0.0), jnp.where(lane3 >= 16, db, da)
        return down, up

    def solve3(cycle):
        s = [[SG[cycle, pl.ds(2 * c + h, 24, stride=8)] for h in range(2)] for c in range(3)]
        for h in range(2):
            new = sym([I3[f, h] for f in range(6)], [s[c][h] for c in range(3)])
            for c in range(3):
                V3[c, h] = new[c]

        def body(i):
            v = [[V3[c, h] for h in range(2)] for c in range(3)]
            p = [[None, None] for c in range(3)]
            for c in range(3):
                down, up = shifts3(v[c][0], v[c][1])
                for h in range(2):
                    a = v[c][h]
                    n = roll(a, 1, 0) + roll(a, -1, 0) + down[h] + up[h]
                    n = n + jnp.where((lane3 & 15) == 0, 0.0, roll(a, 1, 1))
                    n = n + jnp.where((lane3 & 15) == 15, 0.0, roll(a, -1, 1))
                    p[c][h] = SG[cycle, pl.ds(2 * c + h, 24, stride=8)] + W[3] * n
            for h in range(2):
                new = sym([I3[f, h] for f in range(6)], [p[c][h] for c in range(3)])
                for c in range(3):
                    V3[c, h] = KEEP * v[c][h] + new[c]

        loop(0, 7, body)

    def spread3():
        for c in range(3):
            a, b = V3[c, 0], V3[c, 1]
            down, up = shifts3(a, b)
            for h, v in enumerate((a, b)):
                even = 0.75 * v + 0.25 * down[h]
                odd = 0.75 * v + 0.25 * up[h]
                E3[0, pl.ds(32 * c + h, 16, stride=2)] = even[8:24]
                E3[1, pl.ds(32 * c + h, 16, stride=2)] = odd[8:24]
        fine = split_dot(E3[0], M32[0]) + split_dot(E3[1], M32[1])
        for q in range(4):
            P3[pl.ds(q, 96, stride=4)] = fine[:, 128 * q:128 * q + 128]
        for c in range(3):
            def planes(i):
                return P3[128 * c + 8 * i:128 * c + 8 * i + 56].reshape(7, 8, 128)

            before, mid, after = planes(0), planes(1), planes(2)
            even = 0.75 * mid + 0.25 * before
            odd = 0.75 * mid + 0.25 * after
            for i in range(7):
                y = 2 + 2 * i
                V2B[c, y] = (V2B[c, y] + even[i]) * YM2[y]
                V2B[c, y + 1] = (V2B[c, y + 1] + odd[i]) * YM2[y + 1]

    def spread2():
        for c in range(3):
            v = V2B[c, 4:14].reshape(80, 128)
            xm, xp = shifts2(v)
            E21[0, 8 + 80 * c:88 + 80 * c] = 0.75 * v + 0.25 * xm
            E21[1, 8 + 80 * c:88 + 80 * c] = 0.75 * v + 0.25 * xp
        lines = []
        for j in range(3):
            inside = jnp.where((gx + j >= 1) & (gx + j <= 8), 1.0, 0.0).astype(F32)
            for eo in range(2):
                lines.append(E21[eo, pl.ds(7 + gx + j, 32, stride=8)] * inside)
        fine = split_dot(jnp.concatenate(lines, axis=0), M21[...])
        for j in range(3):
            for eo in range(2):
                for q in range(4):
                    at0 = 32 * (2 * j + eo)
                    P21[pl.ds(8 * j + 2 * q + eo, 32, stride=24)] = fine[at0:at0 + 32, 128 * q:128 * q + 128]

        def body(p):
            for c in range(3):
                def lines_of(i):
                    return P21[pl.ds(pl.multiple_of((10 * c + i) * 24, 8), 24)]

                mid = 0.75 * lines_of(p)
                even = mid + 0.25 * lines_of(p - 1)
                odd = mid + 0.25 * lines_of(p + 1)
                V1B[c, 2 * p] = (V1B[c, 2 * p] + even) * (XM1[...] * ym1(2 * p))
                V1B[c, 2 * p + 1] = (V1B[c, 2 * p + 1] + odd) * (XM1[...] * ym1(2 * p + 1))

        loop(1, 9, body)

    def spread1(first, last):
        for c in range(3):
            CZ[c] = split_dot(V1B[c, 4:16].reshape(288, 128), M10[...]).reshape(12, 24, 128)

        def body(p):
            for b in range(2):
                y = 2 * p - 1 + b
                m = XM0[...] * ym0(y)
                for c in range(3):
                    a = 0.75 * CZ[c, p] + 0.25 * CZ[c, p - 1 + 2 * b]
                    mid = 0.75 * roll(a, -4, 0)
                    TMP[b, c, pl.ds(0, 16, stride=2)] = (mid + 0.25 * roll(a, -3, 0))[0:16]
                    TMP[b, c, pl.ds(1, 16, stride=2)] = (mid + 0.25 * roll(a, -5, 0))[0:16]
                    VB[c, y] = (VB[c, y] + TMP[b, c]) * m

        loop(first, last, body)

    for cycle in range(2):
        if cycle == 0:
            loop(4, 18, start0)
            sweep0(VA, VB, 5, 17)
        else:
            sweep0(VB, VA, 4, 18)
            sweep0(VA, VB, 5, 17)
        residue0(VB)
        source1(cycle)
        s1 = {
            peer: send(RS1.at[cycle, 2, 1], RS1.at[cycle, 2 - peer[0], 1 - peer[1]], peer) for peer in BOX
        }
        sent += list(s1.values())

        if cycle == 0:
            received(a2_x)
            rows = []
            for f in range(6):
                one = XA[pl.ds(2 * f, 8, stride=16)]
                two = XA[pl.ds(2 * f + 1, 8, stride=16)]
                A2[f, 8] = one
                A2[f, 9] = two
                rows.append(one + two)
            RA3[192:208] = pack(split_dot(jnp.concatenate(rows, axis=0), P23[...]), 4)
            a2 = [send(A2.at[:, 8:10], A2.at[:, 8 - 2 * d:10 - 2 * d], (d, 0)) for d in RING4]
            a3 = [send(RA3.at[192:208], RA3.at[192 - 16 * d:208 - 16 * d], (d, 0)) for d in RING11]
            sent += a2 + a3
            received(a1_in.values())
            loop(0, 5, functools.partial(unpack, RA1, A1, low6))
            loop(0, 20, inverse1)

        received([s1[peer] for peer in NEAR])
        loop(1, 4, functools.partial(unpack, RS1.at[cycle], S1, low4))
        loop(5, 15, start1)
        sweep1(V1A, V1B, 6, 14)
        residue1(V1B)
        source2(cycle)
        own = pl.ds(pl.multiple_of(gx * 8, 8), 8)
        s2_x = [send(XG.at[cycle, own], XG.at[cycle, own], (0, d)) for d in range(1, 8)]
        sent += s2_x

        received([s1[peer] for peer in OUTER])
        for group in (0, 4):
            unpack(RS1.at[cycle], S1, low4, group)
        loop(1, 5, start1)
        loop(15, 19, start1)
        sweep1(V1A, V1B, 2, 6)
        sweep1(V1A, V1B, 14, 18)

        received(s2_x)
        for c in range(3):
            for j in range(2):
                S2[cycle, c, 8 + j] = XG[cycle, pl.ds(2 * c + j, 8, stride=8)]
        s2 = [send(S2.at[cycle, :, 8:10], S2.at[cycle, :, 8 - 2 * d:10 - 2 * d], (d, 0)) for d in RING4]
        sent += s2
        if cycle == 0:
            received(a2)
            m = damped_inverse([A2[f] for f in range(6)], W[2], YM2[...])
            for f in range(6):
                I2[f] = m[f]
        received(s2[:4])
        start2(cycle, 5, 13)
        sweep2(cycle, V2A, V2B, 6, 12)
        source3(cycle)
        s3 = [send(SG.at[cycle, 96:104], SG.at[cycle, 96 - 8 * d:104 - 8 * d], (d, 0)) for d in RING11]
        sent += s3

        received(s2[4:])
        start2(cycle, 1, 5)
        start2(cycle, 13, 17)
        sweep2(cycle, V2A, V2B, 2, 6)
        sweep2(cycle, V2A, V2B, 12, 16)
        if cycle == 0:
            received(far_in)
            loop(0, 4, start0)
            loop(18, 22, start0)
            sweep0(VA, VB, 1, 5)
            sweep0(VA, VB, 17, 21)
            received(a3)
            place = iota((24, 128), 0) + (gy - 12)
            mask = jnp.where((place >= 0) & (place < 32), 1.0, 0.0)
            for h in range(2):
                m = damped_inverse([RA3[pl.ds(2 * f + h, 24, stride=16)] for f in range(6)], W[3], mask)
                for f in range(6):
                    I3[f, h] = m[f]
        for copy in sent:
            copy.wait_send()
        sent = []

        received(s3)
        solve3(cycle)
        spread3()
        sweep2(cycle, V2B, V2A, 3, 15)
        sweep2(cycle, V2A, V2B, 4, 14)
        spread2()
        sweep1(V1B, V1A, 3, 17)
        sweep1(V1A, V1B, 4, 16)
        if cycle == 0:
            spread1(1, 11)
            sweep0(VB, VA, 2, 20)
            sweep0(VA, VB, 3, 19)
        else:
            spread1(3, 9)
            sweep0(VB, VA, 6, 16)

            def last(y):
                new = swept0(VA, y)
                for c in range(3):
                    out[c, y - 7] = new[c][8:24]

            loop(7, 15, last)


TRANSFERS = 8 + 7 + 14 + 6 + 8 + 22 + 2 * (14 + 7 + 8 + 22)


def local(spatial_grad, temporal_grad):
    def v(*shape, dtype=F32):
        return pltpu.VMEM(shape, dtype)

    def m(*shape):
        return pltpu.VMEM(shape, BF16)

    scratch = [
        v(4, 22, 32, 128), v(22, 32, 128), v(3, 22, 32, 128), v(3, 22, 32, 128), v(3, 10, 32, 128),
        v(32, 128), v(6, 32, 128), v(3, 12, 24, 128), v(2, 3, 32, 128),
        v(5, 3, 6, 2, 8, 128), v(6, 20, 24, 128), v(6, 20, 24, 128), v(2, 5, 3, 3, 2, 8, 128), v(3, 20, 24, 128),
        v(3, 20, 24, 128), v(3, 20, 24, 128), v(3, 6, 24, 128), v(24, 128),
        v(192, 128), v(192, 128), v(128, 128), v(128, 128), v(6, 18, 8, 128), v(6, 18, 8, 128), v(2, 64, 128),
        v(2, 3, 18, 8, 128), v(3, 18, 8, 128), v(3, 18, 8, 128), v(18, 8, 128), v(2, 272, 128), v(768, 128),
        v(384, 128), v(6, 2, 24, 128), v(2, 192, 128), v(3, 2, 24, 128), v(2, 96, 128), v(384, 128),
        m(128, 128), m(128, 128), m(128, 128), m(128, 128), m(128, 128), m(128, 128),
        m(2, 128, 512), m(128, 512), m(128, 128),
        pltpu.SemaphoreType.DMA((2,)),
        pltpu.SemaphoreType.DMA((TRANSFERS,)),
        pltpu.SemaphoreType.DMA((TRANSFERS,)),
    ]
    return pl.pallas_call(
        kernel,
        out_shape=jax.ShapeDtypeStruct(spatial_grad.shape, F32),
        in_specs=[pl.BlockSpec(memory_space=pl.ANY)] * 2,
        out_specs=pl.BlockSpec(memory_space=pltpu.VMEM),
        scratch_shapes=scratch,
        compiler_params=pltpu.CompilerParams(
            collective_id=0, has_side_effects=True, vmem_limit_bytes=48 * 2**20
        ),
        name="flow",
    )(spatial_grad, temporal_grad)


def solution(mesh):
    placed = (P(None, "gy", "gx", None), P("gy", "gx", None))
    return jax.shard_map(
        local, mesh=mesh, in_specs=placed, out_specs=P(None, "gy", "gx", None), check_vma=False
    )
```

profile of v0, /device:TPU:1, one launch (start us, length us, event | category | flops | bytes accessed | tf_op | source)
XLA Modules:
  0.0 110.8 jit_solution(9620120587567345244)
XLA Ops:
  0.0 0.0 copy-start
  0.0 0.9 copy-done
  0.9 0.0 copy-start.1
  0.9 0.8 copy-done.1
  1.8 108.3 %flow.1 = f32[3,8,16,128]{3,2,1,0:T(8,128)S(1)} custom-call(f32[3,8,16,128]{3,2,1,0:T(8,128)S(1)} %copy-done, f32[8,16,128]{2,1,0:T(8,128)S(1)} %copy-done.1), custom_call_target="tpu_custom_call" | custom-call | tf_op jit(solution)/shard_map/flow/pallas_call | solution.py:658
  110.1 0.7 copy.4
Async XLA Ops:
  0.0 0.9 copy-start
  0.9 0.8 copy-start.1
where the time goes:
time: 111 us
  Pallas kernels  108 us (97%)
  local copies, waits for them, and re-layouts  2.44 us (2%)
    pallas_call x1, Pallas kernels, local(): pl.pallas_call(kernel, out_shape=jax.ShapeDtypeStruct(spatial_grad.shape,...  108 us
    unnamed x5, local copies, waits for them, and re-layouts  2.44 us

commit v1 on v0

--- a/solution.py
+++ b/solution.py
@@ -17,8 +17,8 @@
 NEAR = [(a, b) for a in (-1, 0, 1) for b in (-1, 0, 1) if (a, b) != (0, 0)]
 OUTER = [(a, b) for a in (-2, 2) for b in (-1, 0, 1)]
 BOX = NEAR + OUTER
-RING4 = [1, -1, 2, -2, 3, -3, 4, -4]
-RING11 = [s * d for d in range(1, 12) for s in (1, -1)]
+SHEET = [(a, b) for a in (2, -2, 1, -1, 0) for b in range(8) if (a, b) != (0, 0)]
+RING = [s * d for d in range(1, 12) for s in (1, -1)]
 
 
 def loop(first, last, body):
@@ -26,7 +26,7 @@
         body(i)
         return carry
 
-    lax.fori_loop(first, last, step, 0)
+    lax.fori_loop(first, last, step, 0, unroll=4)
 
 
 def iota(shape, dim):
@@ -89,11 +89,15 @@
     gy = lax.axis_index("gy")
     gx = lax.axis_index("gx")
 
+    core = lax.rem(gx, 2)
+    side = 1 - 2 * core
+    twin = (0, side)
+
     def at(dy, dx):
         return lax.rem(gy + dy + 32, 32), lax.rem(gx + dx + 8, 8)
 
     barrier = pltpu.get_barrier_semaphore()
-    everyone = BOX + [(d, 0) for d in RING11 if abs(d) > 2] + [(0, d) for d in (2, 3, 4, 5, 6)]
+    everyone = SHEET + [(d, 0) for d in RING if abs(d) > 2]
     for peer in everyone:
         pl.semaphore_signal(barrier, inc=1, device_id=at(*peer), device_id_type=MESH)
 
@@ -204,33 +208,32 @@
 
     pl.semaphore_wait(barrier, len(everyone))
 
-    span = {-1: (0, 8, 24), 0: (0, 16, 8), 1: (8, 8, 0)}
-
-    def input_copy(peer, rows):
-        dy, dx = peer
-        x0, width, to = span[dx]
-        if dy == 0:
-            y0, height, y1 = 0, 8, 7
-        elif rows == "near":
-            height = 3
-            y0, y1 = (5, 4) if dy == 1 else (0, 15)
-        else:
-            height = 4
-            y0, y1 = (1, 0) if dy == 1 else (3, 18)
+    def input_copy(peer, rows, columns):
+        (y0, y1, height), (x0, x1, width) = rows, columns
         return send(
             IN.at[:, 7 + y0:7 + y0 + height, 8 + x0:8 + x0 + width],
-            IN.at[:, y1:y1 + height, to:to + width],
+            IN.at[:, y1:y1 + height, x1:x1 + width],
             peer,
         )
 
-    near_in = [input_copy(peer, "near") for peer in NEAR]
-    a2_x = [
-        send(XA.at[pl.ds(pl.multiple_of(gx * 16, 16), 16)], XA.at[pl.ds(pl.multiple_of(gx * 16, 16), 16)], (0, d))
-        for d in range(1, 8)
-    ]
-    a1_in = {peer: send(RA1.at[2, 1], RA1.at[2 - peer[0], 1 - peer[1]], peer) for peer in BOX}
-    far_in = [input_copy(peer, "far") for peer in NEAR if peer[0] != 0]
-    sent += near_in + a2_x + list(a1_in.values()) + far_in
+    y_near = {1: (5, 4, 3), -1: (0, 15, 3)}
+    y_far = {1: (1, 0, 4), -1: (3, 18, 4)}
+    x_near = {1: (13, 5, 3), -1: (0, 24, 3)}
+    x_wide = {1: (9, 1, 7), -1: (0, 24, 7)}
+    x_rest = {1: (9, 1, 4), -1: (3, 27, 4)}
+    x_all = {1: (8, 0, 8), -1: (0, 24, 8)}
+
+    near_in = [input_copy((dy, dx), y_near[dy], x_near[dx]) for dy in (1, -1) for dx in (1, -1)]
+    near_in += [input_copy((dy, 0), y_near[dy], (0, 8, 16)) for dy in (1, -1)]
+    near_in += [input_copy((0, dx), (0, 7, 8), x_all[dx]) for dx in (1, -1)]
+    own_a2 = pl.ds(pl.multiple_of(gx * 16, 16), 16)
+    a2_x = [send(XA.at[own_a2], XA.at[own_a2], (0, d)) for d in range(1, 8)]
+
+    def box_copy(src, dst, peer):
+        return send(src.at[2, 1], dst.at[2 - peer[0], 1 - peer[1]], peer)
+
+    a1_near = [box_copy(RA1, RA1, peer) for peer in NEAR]
+    sent += near_in + a2_x + a1_near
     received(near_in)
 
     lane0 = iota((32, 128), 1)
@@ -365,7 +368,7 @@
         for c in range(3):
             for i in range(2):
                 FS[0, 4 * (2 * c + i):4 * (2 * c + i) + 4] = fold_rows(R1, c, 2 * i, 7, 4)
-        XG[cycle, pl.ds(pl.multiple_of(gx * 8, 8), 8)] = pack(split_dot(FS[0, 0:24], M12[...]), 4)
+        XG[cycle, 2, pl.ds(pl.multiple_of(gx * 8, 8), 8)] = pack(split_dot(FS[0, 0:24], M12[...]), 4)
 
     def shifts2(v):
         lane, r = iota(v.shape, 1), iota(v.shape, 0) & 7
@@ -488,6 +491,7 @@
                     at0 = 32 * (2 * j + eo)
                     P21[pl.ds(8 * j + 2 * q + eo, 32, stride=24)] = fine[at0:at0 + 32, 128 * q:128 * q + 128]
 
+    def add2(first, last):
         def body(p):
             for c in range(3):
                 def lines_of(i):
@@ -499,7 +503,7 @@
                 V1B[c, 2 * p] = (V1B[c, 2 * p] + even) * (XM1[...] * ym1(2 * p))
                 V1B[c, 2 * p + 1] = (V1B[c, 2 * p + 1] + odd) * (XM1[...] * ym1(2 * p + 1))
 
-        loop(1, 9, body)
+        loop(first, last, body)
 
     def spread1(first, last):
         for c in range(3):
@@ -520,6 +524,7 @@
 
     for cycle in range(2):
         if cycle == 0:
+            far_in = [input_copy((dy, 0), y_far[dy], (0, 8, 16)) for dy in (1, -1)]
             loop(4, 18, start0)
             sweep0(VA, VB, 5, 17)
         else:
@@ -527,10 +532,9 @@
             sweep0(VA, VB, 5, 17)
         residue0(VB)
         source1(cycle)
-        s1 = {
-            peer: send(RS1.at[cycle, 2, 1], RS1.at[cycle, 2 - peer[0], 1 - peer[1]], peer) for peer in BOX
-        }
-        sent += list(s1.values())
+        s1 = RS1.at[cycle]
+        s1_near = [box_copy(s1, s1, peer) for peer in NEAR]
+        sent += s1_near
 
         if cycle == 0:
             received(a2_x)
@@ -542,70 +546,110 @@
                 A2[f, 9] = two
                 rows.append(one + two)
             RA3[192:208] = pack(split_dot(jnp.concatenate(rows, axis=0), P23[...]), 4)
-            a2 = [send(A2.at[:, 8:10], A2.at[:, 8 - 2 * d:10 - 2 * d], (d, 0)) for d in RING4]
-            a3 = [send(RA3.at[192:208], RA3.at[192 - 16 * d:208 - 16 * d], (d, 0)) for d in RING11]
-            sent += a2 + a3
-            received(a1_in.values())
-            loop(0, 5, functools.partial(unpack, RA1, A1, low6))
-            loop(0, 20, inverse1)
-
-        received([s1[peer] for peer in NEAR])
-        loop(1, 4, functools.partial(unpack, RS1.at[cycle], S1, low4))
+            a2_y = [
+                send(A2.at[:, 8:10], A2.at[:, pl.ds(8 - 2 * d * side, 2)], (d * side, 0)) for d in (3, 2, 1)
+            ]
+            a2_y.append(
+                send(A2.at[:, pl.ds(9 - core, 1)], A2.at[:, pl.ds(9 - core - 8 * side, 1)], (4 * side, 0))
+            )
+            a3_y = [
+                send(RA3.at[192:208], RA3.at[pl.ds(pl.multiple_of(16 * (12 - d * side), 16), 16)], (d * side, 0))
+                for d in range(1, 12)
+            ]
+            sent += a2_y + a3_y
+            received(a1_near)
+            loop(1, 4, functools.partial(unpack, RA1, A1, low6))
+            loop(4, 16, inverse1)
+
+        received(s1_near)
+        loop(1, 4, functools.partial(unpack, s1, S1, low4))
         loop(5, 15, start1)
         sweep1(V1A, V1B, 6, 14)
         residue1(V1B)
         source2(cycle)
         own = pl.ds(pl.multiple_of(gx * 8, 8), 8)
-        s2_x = [send(XG.at[cycle, own], XG.at[cycle, own], (0, d)) for d in range(1, 8)]
-        sent += s2_x
-
-        received([s1[peer] for peer in OUTER])
-        for group in (0, 4):
-            unpack(RS1.at[cycle], S1, low4, group)
-        loop(1, 5, start1)
-        loop(15, 19, start1)
-        sweep1(V1A, V1B, 2, 6)
-        sweep1(V1A, V1B, 14, 18)
-
-        received(s2_x)
-        for c in range(3):
-            for j in range(2):
-                S2[cycle, c, 8 + j] = XG[cycle, pl.ds(2 * c + j, 8, stride=8)]
-        s2 = [send(S2.at[cycle, :, 8:10], S2.at[cycle, :, 8 - 2 * d:10 - 2 * d], (d, 0)) for d in RING4]
-        sent += s2
+        s2 = {
+            (dy, dx): send(XG.at[cycle, 2, own], XG.at[cycle, 2 - dy, own], (dy, dx)) for dy, dx in SHEET
+        }
+        sent += s2.values()
         if cycle == 0:
-            received(a2)
+            s1_far = [box_copy(s1, s1, peer) for peer in OUTER]
+        else:
+            s1_far = [
+                send(s1.at[2, 1, :, row:row + 1], s1.at[2 - dy, 1 - dx, :, row:row + 1], (dy, dx))
+                for dy, dx in OUTER
+                for row in [1 if dy > 0 else 0]
+            ]
+        sent += s1_far
+        if cycle == 0:
+            a1_far = [box_copy(RA1, RA1, peer) for peer in OUTER]
+            sent += a1_far
+            received(a2_y)
+            a2_swap = pl.ds(1 + 9 * core, 7)
+            a2_y = [send(A2.at[:, a2_swap], A2.at[:, a2_swap], twin)]
+            received(a3_y)
+            a3_swap = pl.ds(pl.multiple_of(16 + 192 * core, 16), 176)
+            a3_y = [send(RA3.at[a3_swap], RA3.at[a3_swap], twin)]
+            sent += a2_y + a3_y
+            received(a2_y)
             m = damped_inverse([A2[f] for f in range(6)], W[2], YM2[...])
             for f in range(6):
                 I2[f] = m[f]
-        received(s2[:4])
+        received(s2.values())
+        for i in range(5):
+            for c in range(3):
+                for j in range(2):
+                    S2[cycle, c, 4 + 2 * i + j] = XG[cycle, i, pl.ds(2 * c + j, 8, stride=8)]
         start2(cycle, 5, 13)
         sweep2(cycle, V2A, V2B, 6, 12)
         source3(cycle)
-        s3 = [send(SG.at[cycle, 96:104], SG.at[cycle, 96 - 8 * d:104 - 8 * d], (d, 0)) for d in RING11]
-        sent += s3
-
-        received(s2[4:])
-        start2(cycle, 1, 5)
-        start2(cycle, 13, 17)
-        sweep2(cycle, V2A, V2B, 2, 6)
-        sweep2(cycle, V2A, V2B, 12, 16)
+        reach = [d for d in RING if abs(d) <= 11 - cycle]
+        s3 = [send(SG.at[cycle, 96:104], SG.at[cycle, 96 - 8 * d:104 - 8 * d], (d, 0)) for d in reach]
+
+        s2_far = [
+            send(S2.at[cycle, :, 8:10], S2.at[cycle, :, pl.ds(8 - 6 * side, 2)], (3 * side, 0))
+        ]
         if cycle == 0:
-            received(far_in)
-            loop(0, 4, start0)
-            loop(18, 22, start0)
-            sweep0(VA, VB, 1, 5)
-            sweep0(VA, VB, 17, 21)
-            received(a3)
+            s2_far.append(
+                send(
+                    S2.at[cycle, :, pl.ds(9 - core, 1)],
+                    S2.at[cycle, :, pl.ds(9 - core - 8 * side, 1)],
+                    (4 * side, 0),
+                )
+            )
+            for dy in (1, -1):
+                for dx in (1, -1):
+                    far_in.append(input_copy((dy, dx), y_far[dy], x_wide[dx]))
+                    far_in.append(input_copy((dy, dx), y_near[dy], x_rest[dx]))
+            sent += far_in
+            received(a3_y)
             place = iota((24, 128), 0) + (gy - 12)
             mask = jnp.where((place >= 0) & (place < 32), 1.0, 0.0)
             for h in range(2):
                 m = damped_inverse([RA3[pl.ds(2 * f + h, 24, stride=16)] for f in range(6)], W[3], mask)
                 for f in range(6):
                     I3[f, h] = m[f]
-        for copy in sent:
-            copy.wait_send()
-        sent = []
+        received(s1_far)
+        for group in (0, 4):
+            unpack(s1, S1, low4, group)
+        received(s2_far)
+        swap = pl.ds(1 + 13 * core, 3) if cycle == 0 else pl.ds(2 + 12 * core, 2)
+        s2_swap = [send(S2.at[cycle, :, swap], S2.at[cycle, :, swap], twin)]
+        if cycle == 1:
+            loop(3, 5, start1)
+            loop(15, 17, start1)
+            sweep1(V1A, V1B, 4, 6)
+            sweep1(V1A, V1B, 14, 16)
+            for copy in sent:
+                copy.wait_send()
+        received(s2_swap)
+        start2(cycle, 1, 5)
+        start2(cycle, 13, 17)
+        sweep2(cycle, V2A, V2B, 2, 6)
+        sweep2(cycle, V2A, V2B, 12, 16)
+        late = s3 + s2_far + s2_swap
+        if cycle == 0:
+            sent += late
 
         received(s3)
         solve3(cycle)
@@ -613,13 +657,31 @@
         sweep2(cycle, V2B, V2A, 3, 15)
         sweep2(cycle, V2A, V2B, 4, 14)
         spread2()
-        sweep1(V1B, V1A, 3, 17)
-        sweep1(V1A, V1B, 4, 16)
         if cycle == 0:
+            received(a1_far)
+            for group in (0, 4):
+                unpack(RA1, A1, low6, group)
+            loop(0, 4, inverse1)
+            loop(16, 20, inverse1)
+            loop(1, 5, start1)
+            loop(15, 19, start1)
+            sweep1(V1A, V1B, 2, 6)
+            sweep1(V1A, V1B, 14, 18)
+            add2(1, 9)
+            sweep1(V1B, V1A, 3, 17)
+            sweep1(V1A, V1B, 4, 16)
+            received(far_in)
+            loop(0, 7, start0)
+            loop(15, 22, start0)
+            sweep0(VA, VB, 1, 8)
+            sweep0(VA, VB, 14, 21)
             spread1(1, 11)
             sweep0(VB, VA, 2, 20)
             sweep0(VA, VB, 3, 19)
         else:
+            add2(2, 8)
+            sweep1(V1B, V1A, 5, 15)
+            sweep1(V1A, V1B, 6, 14)
             spread1(3, 9)
             sweep0(VB, VA, 6, 16)
 
@@ -629,9 +691,11 @@
                     out[c, y - 7] = new[c][8:24]
 
             loop(7, 15, last)
-
-
-TRANSFERS = 8 + 7 + 14 + 6 + 8 + 22 + 2 * (14 + 7 + 8 + 22)
+            for copy in late:
+                copy.wait_send()
+
+
+TRANSFERS = 220
 
 
 def local(spatial_grad, temporal_grad):
@@ -646,7 +710,7 @@
         v(32, 128), v(6, 32, 128), v(3, 12, 24, 128), v(2, 3, 32, 128),
         v(5, 3, 6, 2, 8, 128), v(6, 20, 24, 128), v(6, 20, 24, 128), v(2, 5, 3, 3, 2, 8, 128), v(3, 20, 24, 128),
         v(3, 20, 24, 128), v(3, 20, 24, 128), v(3, 6, 24, 128), v(24, 128),
-        v(192, 128), v(192, 128), v(128, 128), v(128, 128), v(6, 18, 8, 128), v(6, 18, 8, 128), v(2, 64, 128),
+        v(192, 128), v(192, 128), v(128, 128), v(128, 128), v(6, 18, 8, 128), v(6, 18, 8, 128), v(2, 5, 64, 128),
         v(2, 3, 18, 8, 128), v(3, 18, 8, 128), v(3, 18, 8, 128), v(18, 8, 128), v(2, 272, 128), v(768, 128),
         v(384, 128), v(6, 2, 24, 128), v(2, 192, 128), v(3, 2, 24, 128), v(2, 96, 128), v(384, 128),
         m(128, 128), m(128, 128), m(128, 128), m(128, 128), m(128, 128), m(128, 128),
@@ -662,7 +726,7 @@
         out_specs=pl.BlockSpec(memory_space=pltpu.VMEM),
         scratch_shapes=scratch,
         compiler_params=pltpu.CompilerParams(
-            collective_id=0, has_side_effects=True, vmem_limit_bytes=48 * 2**20
+            collective_id=0, has_side_effects=True, vmem_limit_bytes=60 * 2**20
         ),
         name="flow",
     )(spatial_grad, temporal_grad)

time: 111 us -> 89.6 us (0.81)
  Pallas kernels: 108 us -> 87.4 us
    pallas_call x1, Pallas kernels: 108 us -> 87.4 us  [local(): pl.pallas_call(kernel, out_shape=jax.ShapeDtypeStruct(spatial_grad.shape,...]
    unnamed x5 -> x1, local copies, waits for them, and re-layouts: 2.44 us -> 1.62 us
where the time goes in v1:
time: 89.6 us; the launch traced here: 89.1 us
  Pallas kernels  87.4 us (98%)
  local copies, waits for them, and re-layouts  1.62 us (2%)
    pallas_call x1, Pallas kernels, local(): pl.pallas_call(kernel, out_shape=jax.ShapeDtypeStruct(spatial_grad.shape,...  87.4 us

profile of v1, /device:TPU:1, one launch (start us, length us, event | category | flops | bytes accessed | tf_op | source)
XLA Modules:
  0.0 89.1 jit_solution(13929363236613867407)
XLA Ops:
  0.0 87.4 %flow.1 = f32[3,8,16,128]{3,2,1,0:T(8,128)} custom-call(f32[3,8,16,128]{3,2,1,0:T(8,128)} %sg.1, f32[8,16,128]{2,1,0:T(8,128)} %tg.1), custom_call_target="tpu_custom_call" | custom-call | tf_op jit(solution)/shard_map/flow/pallas_call | solution.py:722
  87.5 1.6 %copy.4 = f32[3,8,16,128]{3,2,1,0:T(8,128)} copy(f32[3,8,16,128]{3,2,1,0:T(8,128)} %flow.1) | data formatting | bytes 393216

commit v2 on v1

--- a/solution.py
+++ b/solution.py
@@ -10,6 +10,8 @@
 MESH = pl.DeviceIdType.MESH
 F32 = jnp.float32
 BF16 = jnp.bfloat16
+GROUP = 2
+UNROLL = 8
 KEEP = 0.2
 DAMP = 0.8
 W = (1.0, 0.25, 0.0625, 0.015625)
@@ -26,7 +28,18 @@
         body(i)
         return carry
 
-    lax.fori_loop(first, last, step, 0, unroll=4)
+    lax.fori_loop(first, last, step, 0, unroll=min(UNROLL, last - first))
+
+
+def planes(first, last, compute, store):
+    def body(i):
+        y = first + GROUP * i
+        new = [compute(y + k) for k in range(GROUP)]
+        for k in range(GROUP):
+            store(y + k, new[k])
+
+    assert (last - first) % GROUP == 0
+    loop(0, (last - first) // GROUP, body)
 
 
 def iota(shape, dim):
@@ -96,6 +109,10 @@
     def at(dy, dx):
         return lax.rem(gy + dy + 32, 32), lax.rem(gx + dx + 8, 8)
 
+    S2[...] = jnp.zeros_like(S2)
+    A2[...] = jnp.zeros_like(A2)
+    SG[...] = jnp.zeros_like(SG)
+    RA3[...] = jnp.zeros_like(RA3)
     barrier = pltpu.get_barrier_semaphore()
     everyone = SHEET + [(d, 0) for d in RING if abs(d) > 2]
     for peer in everyone:
@@ -124,6 +141,28 @@
 
     sent = []
 
+    load_g.wait()
+    load_t.wait()
+    pl.semaphore_wait(barrier, len(everyone))
+
+    def input_copy(peer, rows, columns):
+        (y0, y1, height), (x0, x1, width) = rows, columns
+        return send(
+            IN.at[:, 7 + y0:7 + y0 + height, 8 + x0:8 + x0 + width],
+            IN.at[:, y1:y1 + height, x1:x1 + width],
+            peer,
+        )
+
+    y_near = {1: (5, 4, 3), -1: (0, 15, 3)}
+    y_far = {1: (1, 0, 4), -1: (3, 18, 4)}
+    x_near = {1: (13, 5, 3), -1: (0, 24, 3)}
+    x_some = {1: (12, 4, 4), -1: (0, 24, 4)}
+    x_rest = {1: (9, 1, 4), -1: (3, 27, 4)}
+    x_all = {1: (8, 0, 8), -1: (0, 24, 8)}
+
+    near_in = [input_copy((dy, dx), y_near[dy], x_near[dx]) for dy in (1, -1) for dx in (1, -1)]
+    near_in += [input_copy((dy, 0), y_near[dy], (0, 8, 16)) for dy in (1, -1)]
+    near_in += [input_copy((0, dx), (0, 7, 8), x_all[dx]) for dx in (1, -1)]
     def lanes(shape):
         return iota(shape, 0), iota(shape, 1)
 
@@ -156,8 +195,6 @@
     plane = iota((18, 8, 128), 0) + (2 * gy - 8)
     YM2[...] = jnp.where((plane >= 0) & (plane < 64), 1.0, 0.0)
     E21[...] = jnp.zeros_like(E21)
-    SG[:, 0:8] = jnp.zeros((2, 8, 128), F32)
-    RA3[0:16] = jnp.zeros((16, 128), F32)
 
     def ym(first, length, y):
         place = first + y
@@ -180,9 +217,6 @@
         return total
 
     F[...] = jnp.zeros_like(F)
-
-    load_g.wait()
-    load_t.wait()
 
     def own_coeffs(i):
         def products(y):
@@ -206,31 +240,18 @@
     halved = C2[pl.ds(0, 96, stride=2)] + C2[pl.ds(1, 96, stride=2)]
     XA[pl.ds(pl.multiple_of(gx * 16, 16), 16)] = pack(split_dot(halved, P12[...]), 8)
 
-    pl.semaphore_wait(barrier, len(everyone))
-
-    def input_copy(peer, rows, columns):
-        (y0, y1, height), (x0, x1, width) = rows, columns
-        return send(
-            IN.at[:, 7 + y0:7 + y0 + height, 8 + x0:8 + x0 + width],
-            IN.at[:, y1:y1 + height, x1:x1 + width],
-            peer,
-        )
-
-    y_near = {1: (5, 4, 3), -1: (0, 15, 3)}
-    y_far = {1: (1, 0, 4), -1: (3, 18, 4)}
-    x_near = {1: (13, 5, 3), -1: (0, 24, 3)}
-    x_wide = {1: (9, 1, 7), -1: (0, 24, 7)}
-    x_rest = {1: (9, 1, 4), -1: (3, 27, 4)}
-    x_all = {1: (8, 0, 8), -1: (0, 24, 8)}
-
-    near_in = [input_copy((dy, dx), y_near[dy], x_near[dx]) for dy in (1, -1) for dx in (1, -1)]
-    near_in += [input_copy((dy, 0), y_near[dy], (0, 8, 16)) for dy in (1, -1)]
-    near_in += [input_copy((0, dx), (0, 7, 8), x_all[dx]) for dx in (1, -1)]
     own_a2 = pl.ds(pl.multiple_of(gx * 16, 16), 16)
     a2_x = [send(XA.at[own_a2], XA.at[own_a2], (0, d)) for d in range(1, 8)]
 
     def box_copy(src, dst, peer):
         return send(src.at[2, 1], dst.at[2 - peer[0], 1 - peer[1]], peer)
+
+    def outer_copy(buf, peer, cycle):
+        dy, dx = peer
+        rows = slice(0, 2) if cycle == 0 else (slice(1, 2) if dy > 0 else slice(0, 1))
+        wide = 3 if cycle == 0 else 1
+        columns = {1: slice(8 - wide, 8), 0: slice(0, 8), -1: slice(0, wide)}[dx]
+        return send(buf.at[2, 1, :, rows, columns], buf.at[2 - dy, 1 - dx, :, rows, columns], peer)
 
     a1_near = [box_copy(RA1, RA1, peer) for peer in NEAR]
     sent += near_in + a2_x + a1_near
@@ -256,10 +277,13 @@
     def start0(y):
         g = [IN[c, y] for c in range(3)]
         q = XM0[...] * ym0(y) * (DAMP / 6.0) / (6.0 + dot3(g, g))
-        Q[y] = q
         scale = -6.0 * IN[3, y] * q
-        for c in range(3):
-            VA[c, y] = scale * g[c]
+        return q, [scale * g[c] for c in range(3)]
+
+    def store0(y, new):
+        Q[y] = new[0]
+        for c in range(3):
+            VA[c, y] = new[1][c]
 
     def swept0(src, y):
         g = [IN[c, y] for c in range(3)]
@@ -271,23 +295,25 @@
         return [KEEP * v[c] + scale * p[c] - d * g[c] for c in range(3)]
 
     def sweep0(src, dst, first, last):
-        def body(y):
-            new = swept0(src, y)
+        def store(y, new):
             for c in range(3):
                 dst[c, y] = new[c]
 
-        loop(first, last, body)
+        planes(first, last, functools.partial(swept0, src), store)
 
     def residue0(src):
-        def body(y):
+        def compute(y):
             g = [IN[c, y] for c in range(3)]
             v, n = around0(src, y)
             d = IN[3, y] + dot3(g, v)
             m = XM0[...] * ym0(y)
-            for c in range(3):
-                R0[c, y - 6] = m * (n[c] - 6.0 * v[c] - g[c] * d)
-
-        loop(6, 16, body)
+            return [m * (n[c] - 6.0 * v[c] - g[c] * d) for c in range(3)]
+
+        def store(y, new):
+            for c in range(3):
+                R0[c, y - 6] = new[c]
+
+        planes(6, 16, compute, store)
 
     def fold_rows(src, c, y, x, size):
         weights = (1.0, 3.0, 3.0, 1.0)
@@ -303,12 +329,8 @@
         return total
 
     def source1(cycle):
-        def body(i):
-            for c in range(3):
-                C1[pl.ds(c * 32 + 8 * i, 8)] = fold_rows(R0, c, 2 * i, 7, 8)
-
-        loop(0, 4, body)
-        s = split_dot(C1[0:96], M01[...])
+        lines = [fold_rows(R0, c, 2 * i, 7, 8) for c in range(3) for i in range(4)]
+        s = split_dot(jnp.concatenate(lines, axis=0), M01[...])
         for c in range(3):
             for j in range(2):
                 at0 = 32 * c + 8 * j
@@ -345,29 +367,34 @@
             V1A[c, y] = new[c]
 
     def sweep1(src, dst, first, last):
-        def body(y):
+        def compute(y):
             v, n = around1(src, y)
             new = sym([I1[f, y] for f in range(6)], [S1[c, y] + W[1] * n[c] for c in range(3)])
-            for c in range(3):
-                dst[c, y] = KEEP * v[c] + new[c]
-
-        loop(first, last, body)
+            return [KEEP * v[c] + new[c] for c in range(3)]
+
+        def store(y, new):
+            for c in range(3):
+                dst[c, y] = new[c]
+
+        planes(first, last, compute, store)
 
     def residue1(src):
-        def body(y):
+        def compute(y):
             v, n = around1(src, y)
             av = sym([A1[f, y] for f in range(6)], v)
             m = XM1[...] * ym1(y)
-            for c in range(3):
-                R1[c, y - 7] = m * (S1[c, y] + W[1] * (n[c] - 6.0 * v[c]) - av[c])
-
-        loop(7, 13, body)
+            return [m * (S1[c, y] + W[1] * (n[c] - 6.0 * v[c]) - av[c]) for c in range(3)]
+
+        def store(y, new):
+            for c in range(3):
+                R1[c, y - 7] = new[c]
+
+        planes(7, 13, compute, store)
 
     def source2(cycle):
-        rows = []
-        for c in range(3):
-            for i in range(2):
-                FS[0, 4 * (2 * c + i):4 * (2 * c + i) + 4] = fold_rows(R1, c, 2 * i, 7, 4)
+        lines = [fold_rows(R1, c, 2 * i, 7, 4) for i in range(2) for c in range(3)]
+        for k in range(6):
+            FS[0, 4 * k:4 * k + 4] = lines[k]
         XG[cycle, 2, pl.ds(pl.multiple_of(gx * 8, 8), 8)] = pack(split_dot(FS[0, 0:24], M12[...]), 4)
 
     def shifts2(v):
@@ -481,9 +508,9 @@
             E21[1, 8 + 80 * c:88 + 80 * c] = 0.75 * v + 0.25 * xp
         lines = []
         for j in range(3):
-            inside = jnp.where((gx + j >= 1) & (gx + j <= 8), 1.0, 0.0).astype(F32)
+            inside = (gx + j >= 1) & (gx + j <= 8)
             for eo in range(2):
-                lines.append(E21[eo, pl.ds(7 + gx + j, 32, stride=8)] * inside)
+                lines.append(jnp.where(inside, E21[eo, pl.ds(7 + gx + j, 32, stride=8)], 0.0))
         fine = split_dot(jnp.concatenate(lines, axis=0), M21[...])
         for j in range(3):
             for eo in range(2):
@@ -493,6 +520,7 @@
 
     def add2(first, last):
         def body(p):
+            new = []
             for c in range(3):
                 def lines_of(i):
                     return P21[pl.ds(pl.multiple_of((10 * c + i) * 24, 8), 24)]
@@ -500,8 +528,11 @@
                 mid = 0.75 * lines_of(p)
                 even = mid + 0.25 * lines_of(p - 1)
                 odd = mid + 0.25 * lines_of(p + 1)
-                V1B[c, 2 * p] = (V1B[c, 2 * p] + even) * (XM1[...] * ym1(2 * p))
-                V1B[c, 2 * p + 1] = (V1B[c, 2 * p + 1] + odd) * (XM1[...] * ym1(2 * p + 1))
+                new.append((V1B[c, 2 * p] + even) * (XM1[...] * ym1(2 * p)))
+                new.append((V1B[c, 2 * p + 1] + odd) * (XM1[...] * ym1(2 * p + 1)))
+            for c in range(3):
+                V1B[c, 2 * p] = new[2 * c]
+                V1B[c, 2 * p + 1] = new[2 * c + 1]
 
         loop(first, last, body)
 
@@ -510,22 +541,32 @@
             CZ[c] = split_dot(V1B[c, 4:16].reshape(288, 128), M10[...]).reshape(12, 24, 128)
 
         def body(p):
+            lines = []
+            for b in range(2):
+                for c in range(3):
+                    a = 0.75 * CZ[c, p] + 0.25 * CZ[c, p - 1 + 2 * b]
+                    mid = 0.75 * roll(a, -4, 0)
+                    lines.append((mid + 0.25 * roll(a, -3, 0), mid + 0.25 * roll(a, -5, 0)))
+            slot = lax.rem(p, 4)
+            for k in range(6):
+                TMP[slot, k, pl.ds(0, 16, stride=2)] = lines[k][0][0:16]
+                TMP[slot, k, pl.ds(1, 16, stride=2)] = lines[k][1][0:16]
+            new = []
             for b in range(2):
                 y = 2 * p - 1 + b
                 m = XM0[...] * ym0(y)
                 for c in range(3):
-                    a = 0.75 * CZ[c, p] + 0.25 * CZ[c, p - 1 + 2 * b]
-                    mid = 0.75 * roll(a, -4, 0)
-                    TMP[b, c, pl.ds(0, 16, stride=2)] = (mid + 0.25 * roll(a, -3, 0))[0:16]
-                    TMP[b, c, pl.ds(1, 16, stride=2)] = (mid + 0.25 * roll(a, -5, 0))[0:16]
-                    VB[c, y] = (VB[c, y] + TMP[b, c]) * m
+                    new.append((VB[c, y] + TMP[slot, 3 * b + c]) * m)
+            for b in range(2):
+                for c in range(3):
+                    VB[c, 2 * p - 1 + b] = new[3 * b + c]
 
         loop(first, last, body)
 
     for cycle in range(2):
         if cycle == 0:
-            far_in = [input_copy((dy, 0), y_far[dy], (0, 8, 16)) for dy in (1, -1)]
-            loop(4, 18, start0)
+            far_in = []
+            planes(4, 18, start0, store0)
             sweep0(VA, VB, 5, 17)
         else:
             sweep0(VB, VA, 4, 18)
@@ -547,13 +588,21 @@
                 rows.append(one + two)
             RA3[192:208] = pack(split_dot(jnp.concatenate(rows, axis=0), P23[...]), 4)
             a2_y = [
-                send(A2.at[:, 8:10], A2.at[:, pl.ds(8 - 2 * d * side, 2)], (d * side, 0)) for d in (3, 2, 1)
+                send(A2.at[:, 8:10], A2.at[:, pl.ds(8 - 2 * d * side, 2)], (d * side, 0)) for d in (2, 1)
             ]
+            chip = pl.ds(jnp.clip(gx - core - 1, 0, 4), 4)
             a2_y.append(
-                send(A2.at[:, pl.ds(9 - core, 1)], A2.at[:, pl.ds(9 - core - 8 * side, 1)], (4 * side, 0))
+                send(A2.at[:, 8:10, chip], A2.at[:, pl.ds(8 - 6 * side, 2), chip], (3 * side, 0))
+            )
+            a2_y.append(
+                send(
+                    A2.at[:, pl.ds(9 - core, 1), chip],
+                    A2.at[:, pl.ds(9 - core - 8 * side, 1), chip],
+                    (4 * side, 0),
+                )
             )
             a3_y = [
-                send(RA3.at[192:208], RA3.at[pl.ds(pl.multiple_of(16 * (12 - d * side), 16), 16)], (d * side, 0))
+                send(RA3.at[192:204], RA3.at[pl.ds(pl.multiple_of(16 * (12 - d * side), 16), 12)], (d * side, 0))
                 for d in range(1, 12)
             ]
             sent += a2_y + a3_y
@@ -568,21 +617,16 @@
         residue1(V1B)
         source2(cycle)
         own = pl.ds(pl.multiple_of(gx * 8, 8), 8)
-        s2 = {
-            (dy, dx): send(XG.at[cycle, 2, own], XG.at[cycle, 2 - dy, own], (dy, dx)) for dy, dx in SHEET
-        }
-        sent += s2.values()
-        if cycle == 0:
-            s1_far = [box_copy(s1, s1, peer) for peer in OUTER]
-        else:
-            s1_far = [
-                send(s1.at[2, 1, :, row:row + 1], s1.at[2 - dy, 1 - dx, :, row:row + 1], (dy, dx))
-                for dy, dx in OUTER
-                for row in [1 if dy > 0 else 0]
-            ]
+        s2 = []
+        for dy, dx in SHEET:
+            first, size = {2: (3, 3), -2: (0, 3)}.get(dy, (0, 6))
+            rows = pl.ds(pl.multiple_of(gx * 8, 8) + first, size)
+            s2.append(send(XG.at[cycle, 2, rows], XG.at[cycle, 2 - dy, rows], (dy, dx)))
+        sent += s2
+        s1_far = [outer_copy(s1, peer, cycle) for peer in OUTER]
         sent += s1_far
         if cycle == 0:
-            a1_far = [box_copy(RA1, RA1, peer) for peer in OUTER]
+            a1_far = [outer_copy(RA1, peer, cycle) for peer in OUTER]
             sent += a1_far
             received(a2_y)
             a2_swap = pl.ds(1 + 9 * core, 7)
@@ -595,31 +639,39 @@
             m = damped_inverse([A2[f] for f in range(6)], W[2], YM2[...])
             for f in range(6):
                 I2[f] = m[f]
-        received(s2.values())
+        received(s2)
         for i in range(5):
             for c in range(3):
                 for j in range(2):
-                    S2[cycle, c, 4 + 2 * i + j] = XG[cycle, i, pl.ds(2 * c + j, 8, stride=8)]
+                    if (i, j) not in ((0, 0), (4, 1)):
+                        S2[cycle, c, 4 + 2 * i + j] = XG[cycle, i, pl.ds(3 * j + c, 8, stride=8)]
         start2(cycle, 5, 13)
         sweep2(cycle, V2A, V2B, 6, 12)
         source3(cycle)
         reach = [d for d in RING if abs(d) <= 11 - cycle]
-        s3 = [send(SG.at[cycle, 96:104], SG.at[cycle, 96 - 8 * d:104 - 8 * d], (d, 0)) for d in reach]
-
-        s2_far = [
-            send(S2.at[cycle, :, 8:10], S2.at[cycle, :, pl.ds(8 - 6 * side, 2)], (3 * side, 0))
-        ]
+        s3 = [send(SG.at[cycle, 96:102], SG.at[cycle, 96 - 8 * d:102 - 8 * d], (d, 0)) for d in reach]
+
+        s2_far = []
+        beside = pl.ds(jnp.clip(gx - 1, 0, 5), 3)
+        for d in (3, -3, 2, -2, 4, -4):
+            if abs(d) == 3:
+                first, size = 8, 2
+            else:
+                first, size = (8 if d in (2, -4) else 9), 1
+            if abs(d) < 4 or cycle == 0:
+                s2_far.append(
+                    send(
+                        S2.at[cycle, :, first:first + size, beside],
+                        S2.at[cycle, :, first - 2 * d:first - 2 * d + size, beside],
+                        (d, 0),
+                    )
+                )
         if cycle == 0:
-            s2_far.append(
-                send(
-                    S2.at[cycle, :, pl.ds(9 - core, 1)],
-                    S2.at[cycle, :, pl.ds(9 - core - 8 * side, 1)],
-                    (4 * side, 0),
-                )
-            )
+            for dy in (1, -1):
+                far_in.append(input_copy((dy, 0), y_far[dy], (0, 8, 16)))
             for dy in (1, -1):
                 for dx in (1, -1):
-                    far_in.append(input_copy((dy, dx), y_far[dy], x_wide[dx]))
+                    far_in.append(input_copy((dy, dx), y_far[dy], x_some[dx]))
                     far_in.append(input_copy((dy, dx), y_near[dy], x_rest[dx]))
             sent += far_in
             received(a3_y)
@@ -632,9 +684,6 @@
         received(s1_far)
         for group in (0, 4):
             unpack(s1, S1, low4, group)
-        received(s2_far)
-        swap = pl.ds(1 + 13 * core, 3) if cycle == 0 else pl.ds(2 + 12 * core, 2)
-        s2_swap = [send(S2.at[cycle, :, swap], S2.at[cycle, :, swap], twin)]
         if cycle == 1:
             loop(3, 5, start1)
             loop(15, 17, start1)
@@ -642,12 +691,12 @@
             sweep1(V1A, V1B, 14, 16)
             for copy in sent:
                 copy.wait_send()
-        received(s2_swap)
+        received(s2_far)
         start2(cycle, 1, 5)
         start2(cycle, 13, 17)
         sweep2(cycle, V2A, V2B, 2, 6)
         sweep2(cycle, V2A, V2B, 12, 16)
-        late = s3 + s2_far + s2_swap
+        late = s3 + s2_far
         if cycle == 0:
             sent += late
 
@@ -671,10 +720,10 @@
             sweep1(V1B, V1A, 3, 17)
             sweep1(V1A, V1B, 4, 16)
             received(far_in)
-            loop(0, 7, start0)
-            loop(15, 22, start0)
-            sweep0(VA, VB, 1, 8)
-            sweep0(VA, VB, 14, 21)
+            planes(0, 8, start0, store0)
+            planes(14, 22, start0, store0)
+            sweep0(VA, VB, 1, 9)
+            sweep0(VA, VB, 13, 21)
             spread1(1, 11)
             sweep0(VB, VA, 2, 20)
             sweep0(VA, VB, 3, 19)
@@ -685,12 +734,11 @@
             spread1(3, 9)
             sweep0(VB, VA, 6, 16)
 
-            def last(y):
-                new = swept0(VA, y)
+            def last(y, new):
                 for c in range(3):
                     out[c, y - 7] = new[c][8:24]
 
-            loop(7, 15, last)
+            planes(7, 15, functools.partial(swept0, VA), last)
             for copy in late:
                 copy.wait_send()
 
@@ -707,7 +755,7 @@
 
     scratch = [
         v(4, 22, 32, 128), v(22, 32, 128), v(3, 22, 32, 128), v(3, 22, 32, 128), v(3, 10, 32, 128),
-        v(32, 128), v(6, 32, 128), v(3, 12, 24, 128), v(2, 3, 32, 128),
+        v(32, 128), v(6, 32, 128), v(3, 12, 24, 128), v(4, 6, 32, 128),
         v(5, 3, 6, 2, 8, 128), v(6, 20, 24, 128), v(6, 20, 24, 128), v(2, 5, 3, 3, 2, 8, 128), v(3, 20, 24, 128),
         v(3, 20, 24, 128), v(3, 20, 24, 128), v(3, 6, 24, 128), v(24, 128),
         v(192, 128), v(192, 128), v(128, 128), v(128, 128), v(6, 18, 8, 128), v(6, 18, 8, 128), v(2, 5, 64, 128),

time: 89.6 us -> 77.2 us (0.86)
  Pallas kernels: 87.4 us -> 75.5 us
    pallas_call x1, Pallas kernels: 87.4 us -> 75.5 us  [local(): pl.pallas_call(kernel, out_shape=jax.ShapeDtypeStruct(spatial_grad.shape,...]
where the time goes in v2:
time: 77.2 us; the launch traced here: 77.1 us
  Pallas kernels  75.5 us (98%)
  local copies, waits for them, and re-layouts  1.62 us (2%)
    pallas_call x1, Pallas kernels, local(): pl.pallas_call(kernel, out_shape=jax.ShapeDtypeStruct(spatial_grad.shape,...  75.5 us
    unnamed x1, local copies, waits for them, and re-layouts  1.62 us

profile of v2, /device:TPU:1, one launch (start us, length us, event | category | flops | bytes accessed | tf_op | source)
XLA Modules:
  0.0 77.1 jit_solution(16805202111611644792)
XLA Ops:
  0.0 75.5 %flow.1 = f32[3,8,16,128]{3,2,1,0:T(8,128)} custom-call(f32[3,8,16,128]{3,2,1,0:T(8,128)} %sg.1, f32[8,16,128]{2,1,0:T(8,128)} %tg.1), custom_call_target="tpu_custom_call" | custom-call | tf_op jit(solution)/shard_map/flow/pallas_call | solution.py:770
  75.5 1.6 %copy.4 = f32[3,8,16,128]{3,2,1,0:T(8,128)} copy(f32[3,8,16,128]{3,2,1,0:T(8,128)} %flow.1) | data formatting | bytes 393216

commit v3 on v2

--- a/solution.py
+++ b/solution.py
@@ -11,7 +11,7 @@
 F32 = jnp.float32
 BF16 = jnp.bfloat16
 GROUP = 2
-UNROLL = 8
+UNROLL = 16
 KEEP = 0.2
 DAMP = 0.8
 W = (1.0, 0.25, 0.0625, 0.015625)
@@ -19,8 +19,8 @@
 NEAR = [(a, b) for a in (-1, 0, 1) for b in (-1, 0, 1) if (a, b) != (0, 0)]
 OUTER = [(a, b) for a in (-2, 2) for b in (-1, 0, 1)]
 BOX = NEAR + OUTER
-SHEET = [(a, b) for a in (2, -2, 1, -1, 0) for b in range(8) if (a, b) != (0, 0)]
-RING = [s * d for d in range(1, 12) for s in (1, -1)]
+SHEET = [(a, b) for a in (2, -2, 1, -1, 0) for b in (4, 3, 5, 2, 6, 1, 7, 0) if (a, b) != (0, 0)]
+RING = [s * d for d in (11, 4, 5, 3, 10, 6, 2, 9, 7, 1, 8) for s in (1, -1)]
 
 
 def loop(first, last, body):
@@ -102,6 +102,11 @@
     gy = lax.axis_index("gy")
     gx = lax.axis_index("gx")
 
+    load_g = pltpu.make_async_copy(sg, IN.at[0:3, 7:15, 8:24], lsem.at[0])
+    load_t = pltpu.make_async_copy(tg, IN.at[3, 7:15, 8:24], lsem.at[1])
+    load_g.start()
+    load_t.start()
+
     core = lax.rem(gx, 2)
     side = 1 - 2 * core
     twin = (0, side)
@@ -117,11 +122,6 @@
     everyone = SHEET + [(d, 0) for d in RING if abs(d) > 2]
     for peer in everyone:
         pl.semaphore_signal(barrier, inc=1, device_id=at(*peer), device_id_type=MESH)
-
-    load_g = pltpu.make_async_copy(sg, IN.at[0:3, 7:15, 8:24], lsem.at[0])
-    load_t = pltpu.make_async_copy(tg, IN.at[3, 7:15, 8:24], lsem.at[1])
-    load_g.start()
-    load_t.start()
 
     count = [0]
 
@@ -155,6 +155,8 @@
 
     y_near = {1: (5, 4, 3), -1: (0, 15, 3)}
     y_far = {1: (1, 0, 4), -1: (3, 18, 4)}
+    y_mid = {1: (3, 2, 2), -1: (3, 18, 2)}
+    y_end = {1: (1, 0, 2), -1: (5, 20, 2)}
     x_near = {1: (13, 5, 3), -1: (0, 24, 3)}
     x_some = {1: (12, 4, 4), -1: (0, 24, 4)}
     x_rest = {1: (9, 1, 4), -1: (3, 27, 4)}
@@ -536,10 +538,11 @@
 
         loop(first, last, body)
 
+    def widen1():
+        for c in range(3):
+            CZ[c] = split_dot(V1B[c, 4:16].reshape(288, 128), M10[...]).reshape(12, 24, 128)
+
     def spread1(first, last):
-        for c in range(3):
-            CZ[c] = split_dot(V1B[c, 4:16].reshape(288, 128), M10[...]).reshape(12, 24, 128)
-
         def body(p):
             lines = []
             for b in range(2):
@@ -565,7 +568,7 @@
 
     for cycle in range(2):
         if cycle == 0:
-            far_in = []
+            far_in = [input_copy((dy, 0), y_mid[dy], (0, 8, 16)) for dy in (1, -1)]
             planes(4, 18, start0, store0)
             sweep0(VA, VB, 5, 17)
         else:
@@ -668,7 +671,7 @@
                 )
         if cycle == 0:
             for dy in (1, -1):
-                far_in.append(input_copy((dy, 0), y_far[dy], (0, 8, 16)))
+                far_in.append(input_copy((dy, 0), y_end[dy], (0, 8, 16)))
             for dy in (1, -1):
                 for dx in (1, -1):
                     far_in.append(input_copy((dy, dx), y_far[dy], x_some[dx]))
@@ -691,17 +694,17 @@
             sweep1(V1A, V1B, 14, 16)
             for copy in sent:
                 copy.wait_send()
+        late = s3 + s2_far
+        if cycle == 0:
+            sent += late
+
+        received(s3)
+        solve3(cycle)
         received(s2_far)
         start2(cycle, 1, 5)
         start2(cycle, 13, 17)
         sweep2(cycle, V2A, V2B, 2, 6)
         sweep2(cycle, V2A, V2B, 12, 16)
-        late = s3 + s2_far
-        if cycle == 0:
-            sent += late
-
-        received(s3)
-        solve3(cycle)
         spread3()
         sweep2(cycle, V2B, V2A, 3, 15)
         sweep2(cycle, V2A, V2B, 4, 14)
@@ -719,6 +722,7 @@
             add2(1, 9)
             sweep1(V1B, V1A, 3, 17)
             sweep1(V1A, V1B, 4, 16)
+            widen1()
             received(far_in)
             planes(0, 8, start0, store0)
             planes(14, 22, start0, store0)
@@ -731,6 +735,7 @@
             add2(2, 8)
             sweep1(V1B, V1A, 5, 15)
             sweep1(V1A, V1B, 6, 14)
+            widen1()
             spread1(3, 9)
             sweep0(VB, VA, 6, 16)
 
@@ -769,12 +774,12 @@
     ]
     return pl.pallas_call(
         kernel,
-        out_shape=jax.ShapeDtypeStruct(spatial_grad.shape, F32),
+        out_shape=pltpu.VMEM(spatial_grad.shape, F32),
         in_specs=[pl.BlockSpec(memory_space=pl.ANY)] * 2,
         out_specs=pl.BlockSpec(memory_space=pltpu.VMEM),
         scratch_shapes=scratch,
         compiler_params=pltpu.CompilerParams(
-            collective_id=0, has_side_effects=True, vmem_limit_bytes=60 * 2**20
+            collective_id=0, has_side_effects=True, vmem_limit_bytes=56 * 2**20
         ),
         name="flow",
     )(spatial_grad, temporal_grad)

time: 77.2 us -> 73.5 us (0.952)
  Pallas kernels: 75.5 us -> 72.7 us
  local copies, waits for them, and re-layouts: 1.62 us -> 0.68 us
    pallas_call x1, Pallas kernels: 75.5 us -> 72.7 us  [local(): pl.pallas_call(kernel, out_shape=pltpu.VMEM(spatial_grad.shape, F32), in_...]
    unnamed x1, local copies, waits for them, and re-layouts: 1.62 us -> 0.68 us
where the time goes in v3:
time: 73.5 us; the launch traced here: 73.4 us
  Pallas kernels  72.7 us (99%)
    pallas_call x1, Pallas kernels, local(): pl.pallas_call(kernel, out_shape=pltpu.VMEM(spatial_grad.shape, F32), in_...  72.7 us

profile of v3, /device:TPU:1, one launch (start us, length us, event | category | flops | bytes accessed | tf_op | source)
XLA Modules:
  0.0 73.4 jit_solution(84485757630690679)
XLA Ops:
  0.0 72.7 %flow.1 = f32[3,8,16,128]{3,2,1,0:T(8,128)S(1)} custom-call(f32[3,8,16,128]{3,2,1,0:T(8,128)} %sg.1, f32[8,16,128]{2,1,0:T(8,128)} %tg.1), custom_call_target="tpu_custom_call" | custom-call | tf_op jit(solution)/shard_map/flow/pallas_call | solution.py:775
  72.7 0.7 copy.4

commit v4 on v3

--- a/solution.py
+++ b/solution.py
@@ -119,7 +119,7 @@
     SG[...] = jnp.zeros_like(SG)
     RA3[...] = jnp.zeros_like(RA3)
     barrier = pltpu.get_barrier_semaphore()
-    everyone = SHEET + [(d, 0) for d in RING if abs(d) > 2]
+    everyone = [(d, 0) for d in RING if abs(d) > 2] + SHEET
     for peer in everyone:
         pl.semaphore_signal(barrier, inc=1, device_id=at(*peer), device_id_type=MESH)
 
@@ -287,13 +287,14 @@
         for c in range(3):
             VA[c, y] = new[1][c]
 
-    def swept0(src, y):
-        g = [IN[c, y] for c in range(3)]
-        t = IN[3, y]
+    def swept0(src, y, own=slice(0, 32)):
+        g = [IN[c, y, own] for c in range(3)]
+        t = IN[3, y, own]
         v, n = around0(src, y)
+        v, n = [a[own] for a in v], [a[own] for a in n]
         p = [n[c] - t * g[c] for c in range(3)]
-        d = dot3(g, p) * Q[y]
-        scale = XM0[...] * (ym0(y) * (DAMP / 6.0))
+        d = dot3(g, p) * Q[y, own]
+        scale = XM0[own] * (ym0(y) * (DAMP / 6.0))
         return [KEEP * v[c] + scale * p[c] - d * g[c] for c in range(3)]
 
     def sweep0(src, dst, first, last):
@@ -538,9 +539,10 @@
 
         loop(first, last, body)
 
-    def widen1():
-        for c in range(3):
-            CZ[c] = split_dot(V1B[c, 4:16].reshape(288, 128), M10[...]).reshape(12, 24, 128)
+    def widen1(first, last):
+        for c in range(3):
+            lines = V1B[c, 4 + first:4 + last].reshape(-1, 128)
+            CZ[c, first:last] = split_dot(lines, M10[...]).reshape(last - first, 24, 128)
 
     def spread1(first, last):
         def body(p):
@@ -671,11 +673,11 @@
                 )
         if cycle == 0:
             for dy in (1, -1):
-                far_in.append(input_copy((dy, 0), y_end[dy], (0, 8, 16)))
-            for dy in (1, -1):
                 for dx in (1, -1):
                     far_in.append(input_copy((dy, dx), y_far[dy], x_some[dx]))
                     far_in.append(input_copy((dy, dx), y_near[dy], x_rest[dx]))
+            for dy in (1, -1):
+                far_in.append(input_copy((dy, 0), y_end[dy], (0, 8, 16)))
             sent += far_in
             received(a3_y)
             place = iota((24, 128), 0) + (gy - 12)
@@ -687,28 +689,6 @@
         received(s1_far)
         for group in (0, 4):
             unpack(s1, S1, low4, group)
-        if cycle == 1:
-            loop(3, 5, start1)
-            loop(15, 17, start1)
-            sweep1(V1A, V1B, 4, 6)
-            sweep1(V1A, V1B, 14, 16)
-            for copy in sent:
-                copy.wait_send()
-        late = s3 + s2_far
-        if cycle == 0:
-            sent += late
-
-        received(s3)
-        solve3(cycle)
-        received(s2_far)
-        start2(cycle, 1, 5)
-        start2(cycle, 13, 17)
-        sweep2(cycle, V2A, V2B, 2, 6)
-        sweep2(cycle, V2A, V2B, 12, 16)
-        spread3()
-        sweep2(cycle, V2B, V2A, 3, 15)
-        sweep2(cycle, V2A, V2B, 4, 14)
-        spread2()
         if cycle == 0:
             received(a1_far)
             for group in (0, 4):
@@ -719,10 +699,32 @@
             loop(15, 19, start1)
             sweep1(V1A, V1B, 2, 6)
             sweep1(V1A, V1B, 14, 18)
+        else:
+            loop(3, 5, start1)
+            loop(15, 17, start1)
+            sweep1(V1A, V1B, 4, 6)
+            sweep1(V1A, V1B, 14, 16)
+        sent += s3 + s2_far
+        if cycle == 1:
+            for copy in sent:
+                copy.wait_send()
+
+        received(s3)
+        solve3(cycle)
+        received(s2_far)
+        start2(cycle, 1 + cycle, 5)
+        start2(cycle, 13, 17 - cycle)
+        sweep2(cycle, V2A, V2B, 2 + cycle, 6)
+        sweep2(cycle, V2A, V2B, 12, 16 - cycle)
+        spread3()
+        sweep2(cycle, V2B, V2A, 3 + cycle, 15 - cycle)
+        sweep2(cycle, V2A, V2B, 4 + cycle, 14 - cycle)
+        spread2()
+        if cycle == 0:
             add2(1, 9)
             sweep1(V1B, V1A, 3, 17)
             sweep1(V1A, V1B, 4, 16)
-            widen1()
+            widen1(0, 12)
             received(far_in)
             planes(0, 8, start0, store0)
             planes(14, 22, start0, store0)
@@ -735,17 +737,15 @@
             add2(2, 8)
             sweep1(V1B, V1A, 5, 15)
             sweep1(V1A, V1B, 6, 14)
-            widen1()
+            widen1(2, 10)
             spread1(3, 9)
             sweep0(VB, VA, 6, 16)
 
             def last(y, new):
                 for c in range(3):
-                    out[c, y - 7] = new[c][8:24]
-
-            planes(7, 15, functools.partial(swept0, VA), last)
-            for copy in late:
-                copy.wait_send()
+                    out[c, y - 7] = new[c]
+
+            planes(7, 15, functools.partial(swept0, VA, own=slice(8, 24)), last)
 
 
 TRANSFERS = 220

time: 73.5 us -> 73.4 us (level)
  no operation moved by 1% of the time
where the time goes in v4:
time: 73.4 us; the launch traced here: 73.3 us
  Pallas kernels  72.6 us (99%)
    pallas_call x1, Pallas kernels, local(): pl.pallas_call(kernel, out_shape=pltpu.VMEM(spatial_grad.shape, F32), in_...  72.6 us

profile of v4, /device:TPU:1, one launch (start us, length us, event | category | flops | bytes accessed | tf_op | source)
XLA Modules:
  0.0 73.3 jit_solution(9060985653183783157)
XLA Ops:
  0.0 72.6 %flow.1 = f32[3,8,16,128]{3,2,1,0:T(8,128)S(1)} custom-call(f32[3,8,16,128]{3,2,1,0:T(8,128)} %sg.1, f32[8,16,128]{2,1,0:T(8,128)} %tg.1), custom_call_target="tpu_custom_call" | custom-call | tf_op jit(solution)/shard_map/flow/pallas_call | solution.py:775
  72.6 0.7 copy.4
